TPU v7x, 32 devices: a whole 2x2x4 slice. The times are simulated.
32 devices in a mesh: groups: 2 (over y), row: 4 (over x, core), col: 4 (over z).
Axes of the slice: x: 2, y: 2, z: 4, core: 2. Of those that a mesh axis runs over, the one named last changes fastest.
Arguments:
- p_tiles: float32 [192, 512, 128], P(('groups', 'row'), 'col'), parts along dimension 0, may hold values from -0.5 to 0.5
- h_tiles: float32 [384, 512, 128], P(('groups', 'row'), 'col'), parts along dimension 0, may hold values from -6 to 6
- pair_lists: int32 [96, 384], P(('groups', 'row'), 'col'), parts along dimension 0, may hold values from 0 to 47, as said below
- pair_counts: int32 [32, 4], P(('groups', 'row'), 'col'), parts along dimension 0, may hold values from 48 to 96, as said below
Outputs:
- c_tiles: float32 [384, 512, 128], P(('groups', 'row'), 'col'), parts along dimension 0
There are 2 independent parts, one for each index of `groups`. A program takes and returns all parts, laid end to end along the dimension named above; each array names one. Nothing has to cross between parts.
Inputs may be any that keep to these rules, and one draw needn't show every extreme that they name: `pair_lists`: entries of role 0 are slots of P below 24, of role 1 slots of H below 48, of role 2 slots of the product below 48; each role's largest slot is named somewhere. `pair_counts`: in every step some tile has 96 live products.
All inputs are finite; a program needn't handle non-finite values.
Results may differ from a plain program's by a relative error of at most 0.0003.
Values sent between devices are 32-bit elements; how exact they have to be, the bound alone decides.
A program may use at most 128 MiB of HBM per device.

v0:
```python
import jax
import jax.numpy as jnp
from jax import lax
from jax.sharding import PartitionSpec as P

STEPS = 4
CAPC = 48


def from_behind(value, axis, steps):
    count = lax.axis_size(axis)
    pairs = [(source, (source + steps) % count) for source in range(count)]
    return lax.ppermute(value, axis, pairs)


def select_blocks(tile, slots):
    count = tile.shape[0]
    table = (slots[:, None] == lax.broadcasted_iota(jnp.int32, (slots.shape[0], count), 1)).astype(
        jnp.float32
    )
    flat = tile.reshape(count, tile.shape[1] * tile.shape[2])
    picked = jnp.dot(
        table, flat, precision=lax.Precision.HIGHEST, preferred_element_type=jnp.float32
    )
    return picked.reshape(slots.shape[0], tile.shape[1], tile.shape[2])


def stack_products(panel_tile, slab_tile, triples, live_count, accum):
    width = triples.shape[1]
    live_mask = lax.broadcasted_iota(jnp.int32, (width,), 0) < live_count
    left_blocks = select_blocks(panel_tile, triples[0])
    right_blocks = select_blocks(slab_tile, triples[1])
    products = jnp.einsum(
        "pij,pjk->pik",
        left_blocks,
        right_blocks,
        precision=lax.Precision.HIGHEST,
        preferred_element_type=jnp.float32,
    )
    place_rows = lax.broadcasted_iota(jnp.int32, (accum.shape[0], width), 0)
    place_table = jnp.logical_and(place_rows == triples[2][None, :], live_mask[None, :]).astype(
        jnp.float32
    )
    flat_products = products.reshape(width, products.shape[1] * products.shape[2])
    placed = jnp.dot(
        place_table,
        flat_products,
        precision=lax.Precision.HIGHEST,
        preferred_element_type=jnp.float32,
    )
    return accum + placed.reshape(accum.shape)


def shards(p_tiles, h_tiles, pair_lists, pair_counts):
    accum = jnp.zeros((CAPC, p_tiles.shape[1], p_tiles.shape[2]), jnp.float32)
    panel_tile = p_tiles
    slab_tile = h_tiles
    for step_index in range(STEPS):
        if step_index > 0:
            panel_tile = from_behind(panel_tile, "col", -1)
            slab_tile = from_behind(slab_tile, "row", -1)
        triples = pair_lists[3 * step_index : 3 * step_index + 3]
        live_count = pair_counts[step_index, 0]
        accum = stack_products(panel_tile, slab_tile, triples, live_count, accum)
    return accum


def solution(mesh):
    placed = (
        P(("groups", "row"), "col", None),
        P(("groups", "row"), "col", None),
        P(("groups", "row"), "col"),
        P(("groups", "row"), "col"),
    )
    return jax.shard_map(
        shards,
        mesh=mesh,
        in_specs=placed,
        out_specs=P(("groups", "row"), "col", None),
        check_vma=False,
    )
```

profile of v0, /device:TPU:0, one launch (start us, length us, event | category | flops | bytes accessed | tf_op | source)
XLA Modules:
  0.0 194.9 jit_solution(9309424940660090497)
XLA Ops:
  0.0 2.4 %collective-permute-start.1 = (f32[48,128,128]{2,1,0:T(8,128)}, f32[48,128,128]{2,1,0:T(8,128)}, u32[]{:S(2)}, u32[]{:S(2)}) collective-permute-start(f32[48,128,128]{2,1,0:T(8,128)} %param.5), channel_id=1, source_target_pairs={{0,12},{4,0},{8,4},{12,8},{1,13},{5,1},{9,5},{13,9},{2,14},{6,2},{... | collective-permute-start | bytes 9437192 | tf_op jit(solution)/shard_map/ppermute | solution.py:13
  2.4 3.6 %collective-permute-start = (f32[24,128,128]{2,1,0:T(8,128)}, f32[24,128,128]{2,1,0:T(8,128)S(1)}, u32[]{:S(2)}, u32[]{:S(2)}) collective-permute-start(f32[24,128,128]{2,1,0:T(8,128)} %param.4), channel_id=1, source_target_pairs={{0,3},{1,0},{2,1},{3,2},{4,7},{5,4},{6,5},{7,6},{8,11},{9,8},{10,9... | collective-permute-start | bytes 4718600 | tf_op jit(solution)/shard_map/ppermute | solution.py:13
  6.0 1.5 fusion.94
  7.4 0.6 iota_compare_fusion.12
  8.0 0.6 iota_compare_fusion.13
  8.6 0.6 iota_compare_fusion.14
  9.3 28.2 %collective-permute-done.1 = f32[48,128,128]{2,1,0:T(8,128)} collective-permute-done((f32[48,128,128]{2,1,0:T(8,128)}, f32[48,128,128]{2,1,0:T(8,128)}, u32[]{:S(2)}, u32[]{:S(2)}) %collective-permute-start.1) | collective-permute-done | bytes 3145760 | tf_op jit(solution)/shard_map/ppermute | solution.py:13
  37.5 2.1 %collective-permute-start.3 = (f32[48,128,128]{2,1,0:T(8,128)}, f32[48,128,128]{2,1,0:T(8,128)}, u32[]{:S(2)}, u32[]{:S(2)}) collective-permute-start(f32[48,128,128]{2,1,0:T(8,128)} %collective-permute-done.1), channel_id=1, source_target_pairs={{0,12},{4,0},{8,4},{12,8},{1,13},{5,1},{9,5},{13,9},{2,14},{6,2},{... | collective-permute-start | bytes 9437192 | tf_op jit(solution)/shard_map/ppermute | solution.py:13
  39.6 0.6 iota_compare_fusion.15
  40.2 1.0 slice_bitcast_fusion.11
  41.2 4.7 %fusion.47 = f32[96,128,128]{2,0,1:T(8,128)S(1)} fusion(s32[96]{0:T(128)S(1)} %get-tuple-element.14, f32[3,8,128,128]{3,2,1,0:T(8,128)} %bitcast.227), kind=kOutput, calls=%fused_computation.58 | convolution fusion | flops 452987136 | bytes 7864704 | tf_op jit(solution)/shard_map/dot_general | solution.py:22
  46.0 3.9 %collective-permute-start.2 = (f32[24,128,128]{2,1,0:T(8,128)S(1)}, f32[24,128,128]{2,1,0:T(8,128)}, u32[]{:S(2)}, u32[]{:S(2)}) collective-permute-start(f32[24,128,128]{2,1,0:T(8,128)S(1)} %collective-permute-done), channel_id=1, source_target_pairs={{0,3},{1,0},{2,1},{3,2},{4,7},{5,4},{6,5},{7,6},{8,11},{9,8},{10,9... | collective-permute-start | bytes 4718600 | tf_op jit(solution)/shard_map/ppermute | solution.py:13
  49.9 4.6 %fusion.33 = f32[96,128,128]{2,0,1:T(8,128)S(1)} fusion(s32[96]{0:T(128)S(1)} %get-tuple-element.13, f32[6,8,128,128]{3,2,1,0:T(8,128)S(1)} %bitcast.226), kind=kOutput, calls=%fused_computation.41 | convolution fusion | flops 905974272 | bytes 9437568 | tf_op jit(solution)/shard_map/dot_general | solution.py:22
  54.5 15.7 %fusion.21 = f32[96,128,128]{2,1,0:T(8,128)S(1)} fusion(f32[96,128,128]{2,0,1:T(8,128)S(1)} %fusion.33, f32[96,128,128]{2,0,1:T(8,128)S(1)} %fusion.47), kind=kOutput, calls=%fused_computation.25 | convolution fusion | flops 2415919104 | bytes 18874368 | tf_op jit(solution)/shard_map/pij,pjk->pik/dot_general | solution.py:33
  70.1 3.4 %fusion.44 = f32[96,128,128]{2,0,1:T(8,128)S(1)} fusion(s32[96]{0:T(128)S(1)} %get-tuple-element.11, f32[3,8,128,128]{3,2,1,0:T(8,128)S(1)} %bitcast.228), kind=kOutput, calls=%fused_computation.55 | convolution fusion | flops 452987136 | bytes 7864704 | tf_op jit(solution)/shard_map/dot_general | solution.py:22
  73.5 9.2 %collective-permute-done.2 = f32[24,128,128]{2,1,0:T(8,128)} collective-permute-done((f32[24,128,128]{2,1,0:T(8,128)S(1)}, f32[24,128,128]{2,1,0:T(8,128)}, u32[]{:S(2)}, u32[]{:S(2)}) %collective-permute-start.2) | collective-permute-done | bytes 1572896 | tf_op jit(solution)/shard_map/ppermute | solution.py:13
  82.7 4.8 %collective-permute-start.4 = (f32[24,128,128]{2,1,0:T(8,128)}, f32[24,128,128]{2,1,0:T(8,128)}, u32[]{:S(2)}, u32[]{:S(2)}) collective-permute-start(f32[24,128,128]{2,1,0:T(8,128)} %collective-permute-done.2), channel_id=1, source_target_pairs={{0,3},{1,0},{2,1},{3,2},{4,7},{5,4},{6,5},{7,6},{8,11},{9,8},{10,9... | collective-permute-start | bytes 4718600 | tf_op jit(solution)/shard_map/ppermute | solution.py:13
  87.5 6.5 %fusion.30 = f32[96,128,128]{2,0,1:T(8,128)S(1)} fusion(s32[96]{0:T(128)S(1)} %get-tuple-element.10, f32[6,8,128,128]{3,2,1,0:T(8,128)} %bitcast.72), kind=kOutput, calls=%fused_computation.38 | convolution fusion | flops 905974272 | bytes 9437568 | tf_op jit(solution)/shard_map/dot_general | solution.py:22
  94.0 4.7 %fusion.41 = f32[96,128,128]{2,0,1:T(8,128)S(1)} fusion(s32[96]{0:T(128)S(1)} %get-tuple-element.8, f32[3,8,128,128]{3,2,1,0:T(8,128)} %bitcast.76), kind=kOutput, calls=%fused_computation.52 | convolution fusion | flops 452987136 | bytes 7864704 | tf_op jit(solution)/shard_map/dot_general | solution.py:22
  98.7 0.2 collective-permute-start.5
  98.9 15.6 %fusion.18 = f32[96,128,128]{2,1,0:T(8,128)S(1)} fusion(f32[96,128,128]{2,0,1:T(8,128)S(1)} %fusion.30, f32[96,128,128]{2,0,1:T(8,128)S(1)} %fusion.44), kind=kOutput, calls=%fused_computation.22 | convolution fusion | flops 2415919104 | bytes 18874368 | tf_op jit(solution)/shard_map/pij,pjk->pik/dot_general | solution.py:33
  114.6 7.8 %fusion.6 = f32[48,128,128]{2,0,1:T(8,128)} fusion(s32[96]{0:T(128)S(1)} %get-tuple-element.12, pred[96]{0:T(512)(128)(4,1)S(1)} %iota_compare_fusion.14, f32[12,8,128,128]{3,2,1,0:T(8,128)S(1)} %bitcast.222), kind=kOutput, calls=%fused_computation.10 | convolution fusion | flops 905978880 | bytes 9437664 | tf_op jit(solution)/shard_map/dot_general | solution.py:45
  122.4 5.1 %fusion.38 = f32[96,128,128]{2,0,1:T(8,128)S(1)} fusion(s32[96]{0:T(128)S(1)} %get-tuple-element.16, f32[3,8,128,128]{3,2,1,0:T(8,128)} %bitcast.82), kind=kOutput, calls=%fused_computation.49 | convolution fusion | flops 452987136 | bytes 7864704 | tf_op jit(solution)/shard_map/dot_general | solution.py:22
  127.5 6.5 %fusion.27 = f32[96,128,128]{2,0,1:T(8,128)S(1)} fusion(s32[96]{0:T(128)S(1)} %get-tuple-element.7, f32[6,8,128,128]{3,2,1,0:T(8,128)} %bitcast.78), kind=kOutput, calls=%fused_computation.35 | convolution fusion | flops 905974272 | bytes 9437568 | tf_op jit(solution)/shard_map/dot_general | solution.py:22
  134.0 15.6 %fusion.15 = f32[96,128,128]{2,1,0:T(8,128)S(1)} fusion(f32[96,128,128]{2,0,1:T(8,128)S(1)} %fusion.27, f32[96,128,128]{2,0,1:T(8,128)S(1)} %fusion.41), kind=kOutput, calls=%fused_computation.19 | convolution fusion | flops 2415919104 | bytes 18874368 | tf_op jit(solution)/shard_map/pij,pjk->pik/dot_general | solution.py:33
  149.6 6.5 %fusion.3 = f32[48,128,128]{2,0,1:T(8,128)S(1)} fusion(s32[96]{0:T(128)S(1)} %get-tuple-element.9, pred[96]{0:T(512)(128)(4,1)S(1)} %iota_compare_fusion.13, f32[12,8,128,128]{3,2,1,0:T(8,128)S(1)} %bitcast.223), kind=kOutput, calls=%fused_computation.7 | convolution fusion | flops 905978880 | bytes 9437664 | tf_op jit(solution)/shard_map/dot_general | solution.py:45
  156.0 6.5 %fusion.24 = f32[96,128,128]{2,0,1:T(8,128)S(1)} fusion(s32[96]{0:T(128)S(1)} %get-tuple-element.15, f32[6,8,128,128]{3,2,1,0:T(8,128)} %bitcast.84), kind=kOutput, calls=%fused_computation.32 | convolution fusion | flops 905974272 | bytes 9437568 | tf_op jit(solution)/shard_map/dot_general | solution.py:22
  162.5 15.8 %fusion.12 = f32[96,128,128]{2,1,0:T(8,128)S(1)} fusion(f32[96,128,128]{2,0,1:T(8,128)S(1)} %fusion.24, f32[96,128,128]{2,0,1:T(8,128)S(1)} %fusion.38), kind=kOutput, calls=%fused_computation.16 | convolution fusion | flops 2415919104 | bytes 18874368 | tf_op jit(solution)/shard_map/pij,pjk->pik/dot_general | solution.py:33
  178.3 0.0 copy-start
  178.3 6.4 %fusion = f32[48,128,128]{2,0,1:T(8,128)S(1)} fusion(s32[96]{0:T(128)S(1)} %get-tuple-element.6, pred[96]{0:T(512)(128)(4,1)S(1)} %iota_compare_fusion.12, f32[12,8,128,128]{3,2,1,0:T(8,128)S(1)} %bitcast.224), kind=kOutput, calls=%fused_computation.4 | convolution fusion | flops 905978880 | bytes 9437664 | tf_op jit(solution)/shard_map/dot_general | solution.py:45
  184.8 7.3 %add_add_fusion = f32[48,128,128]{2,0,1:T(8,128)S(1)} fusion(f32[48,128,128]{2,0,1:T(8,128)S(1)} %fusion, f32[48,128,128]{2,0,1:T(8,128)S(1)} %fusion.3, f32[48,128,128]{2,0,1:T(8,128)S(1)} %copy-done, s32[96]{0:T(128)S(1)} %get-tuple-element.5, pred[96]{0:T(512)(128)(4,1)S(1)} %iota_compare_fusion.15, f32[12,8,128,128]{3,2,1,0:T(8,128)S(1)} %bitcast.225), kind=kOutput, calls=%fused_computation.44 | convolution fusion | flops 908338176 | bytes 18874848 | tf_op jit(solution)/shard_map/dot_general | solution.py:45
  192.1 2.6 %copy.10 = f32[48,128,128]{2,1,0:T(8,128)} copy(f32[48,128,128]{2,0,1:T(8,128)S(1)} %add_add_fusion) | data formatting | bytes 6291456 | tf_op jit(solution)/shard_map/add | solution.py:51
  (7 shorter events, 0.0 us)
Async XLA Ops:
  0.0 49.9 %copy-start.1 = (f32[48,128,128]{2,1,0:T(8,128)S(1)}, f32[48,128,128]{2,1,0:T(8,128)}, u32[]{:S(2)}) copy-start(f32[48,128,128]{2,1,0:T(8,128)} %param.5) | copy-start | bytes 9437188
  0.0 37.5 %collective-permute-start.1 = (f32[48,128,128]{2,1,0:T(8,128)}, f32[48,128,128]{2,1,0:T(8,128)}, u32[]{:S(2)}, u32[]{:S(2)}) collective-permute-start(f32[48,128,128]{2,1,0:T(8,128)} %param.5), channel_id=1, source_target_pairs={{0,12},{4,0},{8,4},{12,8},{1,13},{5,1},{9,5},{13,9},{2,14},{6,2},{... | collective-permute-start | bytes 9437192 | tf_op jit(solution)/shard_map/ppermute | solution.py:13
  2.4 43.6 %collective-permute-start = (f32[24,128,128]{2,1,0:T(8,128)}, f32[24,128,128]{2,1,0:T(8,128)S(1)}, u32[]{:S(2)}, u32[]{:S(2)}) collective-permute-start(f32[24,128,128]{2,1,0:T(8,128)} %param.4), channel_id=1, source_target_pairs={{0,3},{1,0},{2,1},{3,2},{4,7},{5,4},{6,5},{7,6},{8,11},{9,8},{10,9... | collective-permute-start | bytes 4718600 | tf_op jit(solution)/shard_map/ppermute | solution.py:13
  37.5 61.2 %collective-permute-start.3 = (f32[48,128,128]{2,1,0:T(8,128)}, f32[48,128,128]{2,1,0:T(8,128)}, u32[]{:S(2)}, u32[]{:S(2)}) collective-permute-start(f32[48,128,128]{2,1,0:T(8,128)} %collective-permute-done.1), channel_id=1, source_target_pairs={{0,12},{4,0},{8,4},{12,8},{1,13},{5,1},{9,5},{13,9},{2,14},{6,2},{... | collective-permute-start | bytes 9437192 | tf_op jit(solution)/shard_map/ppermute | solution.py:13
  46.0 36.7 %collective-permute-start.2 = (f32[24,128,128]{2,1,0:T(8,128)S(1)}, f32[24,128,128]{2,1,0:T(8,128)}, u32[]{:S(2)}, u32[]{:S(2)}) collective-permute-start(f32[24,128,128]{2,1,0:T(8,128)S(1)} %collective-permute-done), channel_id=1, source_target_pairs={{0,3},{1,0},{2,1},{3,2},{4,7},{5,4},{6,5},{7,6},{8,11},{9,8},{10,9... | collective-permute-start | bytes 4718600 | tf_op jit(solution)/shard_map/ppermute | solution.py:13
  82.7 39.7 %collective-permute-start.4 = (f32[24,128,128]{2,1,0:T(8,128)}, f32[24,128,128]{2,1,0:T(8,128)}, u32[]{:S(2)}, u32[]{:S(2)}) collective-permute-start(f32[24,128,128]{2,1,0:T(8,128)} %collective-permute-done.2), channel_id=1, source_target_pairs={{0,3},{1,0},{2,1},{3,2},{4,7},{5,4},{6,5},{7,6},{8,11},{9,8},{10,9... | collective-permute-start | bytes 4718600 | tf_op jit(solution)/shard_map/ppermute | solution.py:13
  98.7 57.3 %collective-permute-start.5 = (f32[48,128,128]{2,1,0:T(8,128)}, f32[48,128,128]{2,1,0:T(8,128)}, u32[]{:S(2)}, u32[]{:S(2)}) collective-permute-start(f32[48,128,128]{2,1,0:T(8,128)} %collective-permute-done.3), channel_id=1, source_target_pairs={{0,12},{4,0},{8,4},{12,8},{1,13},{5,1},{9,5},{13,9},{2,14},{6,2},{... | collective-permute-start | bytes 9437192 | tf_op jit(solution)/shard_map/ppermute | solution.py:13
  178.3 6.5 %copy-start = (f32[48,128,128]{2,0,1:T(8,128)S(1)}, f32[48,128,128]{2,0,1:T(8,128)}, u32[]{:S(2)}) copy-start(f32[48,128,128]{2,0,1:T(8,128)} %fusion.6) | copy-start | bytes 9437188
where the time goes:
time: 199 us; the launch traced here: 195 us
  matrix products  133 us (67%)
  waiting for transfers between devices  37.4 us (19%)
  starting transfers between devices  17 us (9%)
  local copies, waits for them, and re-layouts  5.08 us (3%)
  other arithmetic  2.48 us (1%)
    dot_general x4, matrix products, stack_products(): jnp.einsum('pij,pjk->pik', left_blocks, right_blocks, precision=lax.Preci...  62.7 us
    dot_general x8, matrix products, select_blocks(): jnp.dot(table, flat, precision=lax.Precision.HIGHEST, preferred_element_t...  41.9 us
    ppermute x6, waiting for transfers between devices, from_behind(): return lax.ppermute(value, axis, pairs)  37.4 us
    dot_general x4, matrix products, stack_products(): jnp.dot(place_table, flat_products, precision=lax.Precision.HIGHEST, pref...  27.9 us
    ppermute x6, starting transfers between devices, from_behind(): return lax.ppermute(value, axis, pairs)  17 us
  transfers between devices with their start and end apart: 6, of which 2 were waited for; matrix products, arithmetic and copies ran while one was open for 52% of the time, Pallas kernels for 0%

commit v1 on v0

v1 whole, which is shorter than its diff:
```python
import functools

import jax
import jax.numpy as jnp
from jax import lax
from jax.experimental import pallas as pl
from jax.experimental.pallas import tpu as pltpu
from jax.sharding import PartitionSpec as P

STEPS = 4
CAPC = 48
GROUP = 4


def from_behind(value, axis, steps):
    count = lax.axis_size(axis)
    pairs = [(source, (source + steps) % count) for source in range(count)]
    return lax.ppermute(value, axis, pairs)


def split(value):
    high = value.astype(jnp.bfloat16)
    low = (value - high.astype(jnp.float32)).astype(jnp.bfloat16)
    return high, low


def split_left(source, target, first, count):
    def body(slot, carry):
        high, low = split(source[slot])
        target[slot, :, 0:128] = high
        target[slot, :, 128:256] = low
        return carry

    lax.fori_loop(first, first + count, body, 0)


def split_right(source, target, first, count):
    def body(slot, carry):
        high, low = split(source[slot])
        target[slot, 0:128, 0:128] = high
        target[slot, 0:128, 128:256] = low
        target[slot, 128:256, 0:128] = high
        return carry

    lax.fori_loop(first, first + count, body, 0)


def clear_corner(target, count):
    def body(slot, carry):
        target[slot, 128:256, 128:256] = jnp.zeros((128, 128), jnp.bfloat16)
        return carry

    lax.fori_loop(0, count, body, 0)


def multiply(left, right):
    both = jnp.dot(left, right, preferred_element_type=jnp.float32)
    return both[:, 0:128] + both[:, 128:256]


def step_kernel(lists, live, left, right, before, after, left_parts, right_parts):
    split_left(left, left_parts, 0, left.shape[0])
    clear_corner(right_parts, right.shape[0])
    split_right(right, right_parts, 0, right.shape[0])
    after[...] = before[...]
    count = live[0]

    def body(group, carry):
        first = group * GROUP
        products = []
        for k in range(GROUP):
            product = multiply(left_parts[lists[0, first + k]], right_parts[lists[1, first + k]])
            products.append(jnp.where(first + k < count, product, 0.0))
        for k in range(GROUP):
            place = lists[2, first + k]
            after[place] = after[place] + products[k]
        return carry

    lax.fori_loop(0, (count + GROUP - 1) // GROUP, body, 0)


def step(left, right, lists, live, before):
    width = lists.shape[1]
    return pl.pallas_call(
        step_kernel,
        out_shape=jax.ShapeDtypeStruct(before.shape, jnp.float32),
        in_specs=[
            pl.BlockSpec(memory_space=pltpu.SMEM),
            pl.BlockSpec(memory_space=pltpu.SMEM),
            pl.BlockSpec(memory_space=pltpu.VMEM),
            pl.BlockSpec(memory_space=pltpu.VMEM),
            pl.BlockSpec(memory_space=pltpu.VMEM),
        ],
        out_specs=pl.BlockSpec(memory_space=pltpu.VMEM),
        scratch_shapes=[
            pltpu.VMEM((left.shape[0], 128, 256), jnp.bfloat16),
            pltpu.VMEM((right.shape[0], 256, 256), jnp.bfloat16),
        ],
        compiler_params=pltpu.CompilerParams(vmem_limit_bytes=40 << 20),
        cost_estimate=pl.CostEstimate(
            flops=width * 2 * 128 * 256 * 256, bytes_accessed=12 << 20, transcendentals=0
        ),
    )(lists, live, left, right, before)


def shards(p_tiles, h_tiles, pair_lists, pair_counts):
    accum = jnp.zeros((CAPC, p_tiles.shape[1], p_tiles.shape[2]), jnp.float32)
    panel_tile = p_tiles
    slab_tile = h_tiles
    for index in range(STEPS):
        if index > 0:
            panel_tile = from_behind(panel_tile, "col", -1)
            slab_tile = from_behind(slab_tile, "row", -1)
        lists = pair_lists[3 * index : 3 * index + 3]
        accum = step(panel_tile, slab_tile, lists, pair_counts[index], accum)
    return accum


def solution(mesh):
    placed = (
        P(("groups", "row"), "col", None),
        P(("groups", "row"), "col", None),
        P(("groups", "row"), "col"),
        P(("groups", "row"), "col"),
    )
    return jax.shard_map(
        shards,
        mesh=mesh,
        in_specs=placed,
        out_specs=P(("groups", "row"), "col", None),
        check_vma=False,
    )
```

time: 199 us -> 160 us (0.80)
  the two profiles are of different devices: /device:TPU:0 before, /device:TPU:30 now
where the time goes in v1:
time: 160 us; the launch traced here: 159 us
  waiting for transfers between devices  120 us (75%)
  Pallas kernels  32.9 us (21%)
  local copies, waits for them, and re-layouts  4.03 us (3%)
  starting transfers between devices  2.26 us (1%)
    ppermute x6, waiting for transfers between devices, from_behind(): return lax.ppermute(value, axis, pairs)  120 us
    pallas_call x4, Pallas kernels, step(): pl.pallas_call(step_kernel, out_shape=jax.ShapeDtypeStruct(before.shape,...  32.9 us
  transfers between devices with their start and end apart: 6, of which 4 were waited for; matrix products, arithmetic and copies ran while one was open for 2% of the time, Pallas kernels for 14%

profile of v1, /device:TPU:30, one launch (start us, length us, event | category | flops | bytes accessed | tf_op | source)
XLA Modules:
  0.0 159.4 jit_solution(1073960076973954501)
XLA Ops:
  0.0 0.0 copy-start
  0.0 0.0 collective-permute-start.3
  0.0 35.2 %collective-permute-done.3.right = f32[48,128,128]{2,1,0:T(8,128)S(1)} collective-permute-done((f32[48,128,128]{2,1,0:T(8,128)}, f32[48,128,128]{2,1,0:T(8,128)S(1)}, u32[]{:S(2)}, u32[]{:S(2)}) %collective-permute-start.3) | collective-permute-done | bytes 3145760 | tf_op jit(solution)/shard_map/ppermute | solution.py:18
  35.2 1.8 %collective-permute-start.4 = (f32[48,128,128]{2,1,0:T(8,128)S(1)}, f32[48,128,128]{2,1,0:T(8,128)S(1)}, u32[]{:S(2)}, u32[]{:S(2)}) collective-permute-start(f32[48,128,128]{2,1,0:T(8,128)S(1)} %collective-permute-done.3.right), channel_id=1, source_target_pairs={{0,12},{4,0},{8,4},{12,8},{1,13},{5,1},{9,5},{13,9},{2,14},{6,2},{... | collective-permute-start | bytes 9437192 | tf_op jit(solution)/shard_map/ppermute | solution.py:18
  37.0 0.4 collective-permute-start
  37.4 37.6 %collective-permute-done.left = f32[24,128,128]{2,1,0:T(8,128)S(1)} collective-permute-done((f32[24,128,128]{2,1,0:T(8,128)}, f32[24,128,128]{2,1,0:T(8,128)S(1)}, u32[]{:S(2)}, u32[]{:S(2)}) %collective-permute-start) | collective-permute-done | bytes 1572896 | tf_op jit(solution)/shard_map/ppermute | solution.py:18
  75.1 0.0 collective-permute-start.1
  75.1 0.0 collective-permute-done.4.right
  75.1 0.0 collective-permute-start.5
  75.1 37.0 %collective-permute-done.1.left = f32[24,128,128]{2,1,0:T(8,128)S(1)} collective-permute-done((f32[24,128,128]{2,1,0:T(8,128)S(1)}, f32[24,128,128]{2,1,0:T(8,128)S(1)}, u32[]{:S(2)}, u32[]{:S(2)}) %collective-permute-start.1) | collective-permute-done | bytes 1572896 | tf_op jit(solution)/shard_map/ppermute | solution.py:18
  112.0 0.0 collective-permute-start.2
  112.0 1.5 fusion.1
  113.5 0.8 fusion
  114.3 0.4 broadcast_in_dim.3.before
  114.7 0.0 copy-done
  114.7 0.0 copy-start.1
  114.7 1.4 copy-done.1
  116.1 7.2 %shard_map.46.before = f32[48,128,128]{2,1,0:T(8,128)S(1)} custom-call(s32[3,96]{1,0:T(4,128)S(1)} %get-tuple-element.5.lists, s32[1]{0:T(128)} %bitcast.3.live, f32[24,128,128]{2,1,0:T(8,128)S(1)} %copy-done.1, f32[48,128,128]{2,1,0:T(8,128)S(1)} %copy-done, f32[48,128,128]{2,1,0:T(8,128)S(1)} %broadcast_in_dim.3.before), custom_call_target="tpu_custom_call" | custom-call | flops 1610612736 | bytes 12582912 | tf_op jit(solution)/shard_map/pallas_call | solution.py:84
  123.3 8.4 %shard_map.47.before = f32[48,128,128]{2,1,0:T(8,128)S(1)} custom-call(s32[3,96]{1,0:T(4,128)S(1)} %get-tuple-element.8.lists, s32[1]{0:T(128)} %bitcast.2.live, f32[24,128,128]{2,1,0:T(8,128)S(1)} %collective-permute-done.left, f32[48,128,128]{2,1,0:T(8,128)S(1)} %collective-permute-done.3.right, f32[48,128,128]{2,1,0:T(8,128)S(1)} %shard_map.46.before), custom_call_target="tpu_custom_call" | custom-call | flops 1610612736 | bytes 12582912 | tf_op jit(solution)/shard_map/pallas_call | solution.py:84
  131.7 6.1 %shard_map.48.before = f32[48,128,128]{2,1,0:T(8,128)S(1)} custom-call(s32[3,96]{1,0:T(4,128)S(1)} %get-tuple-element.6.lists, s32[1]{0:T(128)} %bitcast.1.live, f32[24,128,128]{2,1,0:T(8,128)S(1)} %collective-permute-done.1.left, f32[48,128,128]{2,1,0:T(8,128)S(1)} %collective-permute-done.4.right, f32[48,128,128]{2,1,0:T(8,128)S(1)} %shard_map.47.before), custom_call_target="tpu_custom_call" | custom-call | flops 1610612736 | bytes 12582912 | tf_op jit(solution)/shard_map/pallas_call | solution.py:84
  137.8 10.4 %collective-permute-done.2.left = f32[24,128,128]{2,1,0:T(8,128)} collective-permute-done((f32[24,128,128]{2,1,0:T(8,128)S(1)}, f32[24,128,128]{2,1,0:T(8,128)}, u32[]{:S(2)}, u32[]{:S(2)}) %collective-permute-start.2) | collective-permute-done | bytes 1572896 | tf_op jit(solution)/shard_map/ppermute | solution.py:18
  148.2 0.0 collective-permute-done.5.right
  148.2 11.2 %shard_map.49 = f32[48,128,128]{2,1,0:T(8,128)} custom-call(s32[3,96]{1,0:T(4,128)S(1)} %get-tuple-element.7.lists, s32[1]{0:T(128)} %bitcast.live, f32[24,128,128]{2,1,0:T(8,128)} %collective-permute-done.2.left, f32[48,128,128]{2,1,0:T(8,128)S(1)} %collective-permute-done.5.right, f32[48,128,128]{2,1,0:T(8,128)S(1)} %shard_map.48.before), custom_call_target="tpu_custom_call" | custom-call | flops 1610612736 | bytes 12582912 | tf_op jit(solution)/shard_map/pallas_call | solution.py:84
Async XLA Ops:
  0.0 114.7 %copy-start = (f32[48,128,128]{2,1,0:T(8,128)S(1)}, f32[48,128,128]{2,1,0:T(8,128)}, u32[]{:S(2)}) copy-start(f32[48,128,128]{2,1,0:T(8,128)} %right.1) | copy-start | bytes 9437188
  0.0 35.2 %collective-permute-start.3 = (f32[48,128,128]{2,1,0:T(8,128)}, f32[48,128,128]{2,1,0:T(8,128)S(1)}, u32[]{:S(2)}, u32[]{:S(2)}) collective-permute-start(f32[48,128,128]{2,1,0:T(8,128)} %right.1), channel_id=1, source_target_pairs={{0,12},{4,0},{8,4},{12,8},{1,13},{5,1},{9,5},{13,9},{2,14},{6,2},{... | collective-permute-start | bytes 9437192 | tf_op jit(solution)/shard_map/ppermute | solution.py:18
  35.2 39.9 %collective-permute-start.4 = (f32[48,128,128]{2,1,0:T(8,128)S(1)}, f32[48,128,128]{2,1,0:T(8,128)S(1)}, u32[]{:S(2)}, u32[]{:S(2)}) collective-permute-start(f32[48,128,128]{2,1,0:T(8,128)S(1)} %collective-permute-done.3.right), channel_id=1, source_target_pairs={{0,12},{4,0},{8,4},{12,8},{1,13},{5,1},{9,5},{13,9},{2,14},{6,2},{... | collective-permute-start | bytes 9437192 | tf_op jit(solution)/shard_map/ppermute | solution.py:18
  37.0 38.1 %collective-permute-start = (f32[24,128,128]{2,1,0:T(8,128)}, f32[24,128,128]{2,1,0:T(8,128)S(1)}, u32[]{:S(2)}, u32[]{:S(2)}) collective-permute-start(f32[24,128,128]{2,1,0:T(8,128)} %left.1), channel_id=1, source_target_pairs={{0,3},{1,0},{2,1},{3,2},{4,7},{5,4},{6,5},{7,6},{8,11},{9,8},{10,9... | collective-permute-start | bytes 4718600 | tf_op jit(solution)/shard_map/ppermute | solution.py:18
  75.1 37.0 %collective-permute-start.1 = (f32[24,128,128]{2,1,0:T(8,128)S(1)}, f32[24,128,128]{2,1,0:T(8,128)S(1)}, u32[]{:S(2)}, u32[]{:S(2)}) collective-permute-start(f32[24,128,128]{2,1,0:T(8,128)S(1)} %collective-permute-done.left), channel_id=1, source_target_pairs={{0,3},{1,0},{2,1},{3,2},{4,7},{5,4},{6,5},{7,6},{8,11},{9,8},{10,9... | collective-permute-start | bytes 4718600 | tf_op jit(solution)/shard_map/ppermute | solution.py:18
  75.1 73.1 %collective-permute-start.5 = (f32[48,128,128]{2,1,0:T(8,128)S(1)}, f32[48,128,128]{2,1,0:T(8,128)S(1)}, u32[]{:S(2)}, u32[]{:S(2)}) collective-permute-start(f32[48,128,128]{2,1,0:T(8,128)S(1)} %collective-permute-done.4.right), channel_id=1, source_target_pairs={{0,12},{4,0},{8,4},{12,8},{1,13},{5,1},{9,5},{13,9},{2,14},{6,2},{... | collective-permute-start | bytes 9437192 | tf_op jit(solution)/shard_map/ppermute | solution.py:18
  112.0 36.2 %collective-permute-start.2 = (f32[24,128,128]{2,1,0:T(8,128)S(1)}, f32[24,128,128]{2,1,0:T(8,128)}, u32[]{:S(2)}, u32[]{:S(2)}) collective-permute-start(f32[24,128,128]{2,1,0:T(8,128)S(1)} %collective-permute-done.1.left), channel_id=1, source_target_pairs={{0,3},{1,0},{2,1},{3,2},{4,7},{5,4},{6,5},{7,6},{8,11},{9,8},{10,9... | collective-permute-start | bytes 4718600 | tf_op jit(solution)/shard_map/ppermute | solution.py:18
  114.7 1.4 copy-start.1

commit v2 on v1

--- a/solution.py
+++ b/solution.py
@@ -103,7 +103,214 @@
     )(lists, live, left, right, before)
 
 
+CHUNKS = 4
+MESH = pl.DeviceIdType.MESH
+
+
+def sort_pairs(pair_lists, pair_counts):
+    width = pair_lists.shape[1]
+    triples = pair_lists.reshape(STEPS, 3, width)
+    slot = lax.broadcasted_iota(jnp.int32, (STEPS, width), 1)
+    place = jnp.where(slot < pair_counts, triples[:, 2], CAPC)
+    order = place * width + slot
+    rank = jnp.sum((order[:, None, :] < order[:, :, None]).astype(jnp.int32), axis=2)
+    packed = (triples[:, 0] * 1024 + triples[:, 1]) * 1024 + place
+    hit = rank[:, :, None] == lax.broadcasted_iota(jnp.int32, (STEPS, width, width), 2)
+    ordered = jnp.sum(jnp.where(hit, packed[:, :, None], 0), axis=1)
+    target = ordered % 1024
+    behind = jnp.concatenate([jnp.full((STEPS, 1), -1, jnp.int32), target[:, :-1]], axis=1)
+    keep = (target == behind).astype(jnp.float32)
+    kept = lax.broadcasted_iota(jnp.int32, (STEPS, CAPC, width), 1)
+    last = jnp.sum((place[:, None, :] <= kept).astype(jnp.int32), axis=2) - 1
+    some = jnp.max((place[:, None, :] == kept).astype(jnp.float32), axis=2)
+    slots = jnp.concatenate([ordered // 1048576, ordered // 1024 % 1024], axis=0)
+    return slots, jnp.maximum(last, 0), keep, some
+
+
+def ring_kernel(
+    slots, last, keep, some, p_ref, h_ref, c_ref,
+    panels, slabs, left_parts, right_parts, runs,
+    own_sem, p_left, p_right, p_recv, h_send, h_recv,
+):
+    group = lax.axis_index("groups")
+    row = lax.axis_index("row")
+    col = lax.axis_index("col")
+    count = p_ref.shape[0]
+    piece = count // CHUNKS
+    width = keep.shape[1]
+    sibling = row + 1 - 2 * (row % 2)
+    across = (row + 2) % 4
+    diagonal = (sibling + 2) % 4
+
+    barrier = pltpu.get_barrier_semaphore()
+
+    def greet(r, c):
+        pl.semaphore_signal(barrier, inc=1, device_id=(group, r, c), device_id_type=MESH)
+
+    greet(sibling, col)
+    greet(across, col)
+
+    @pl.when(col > 0)
+    def _():
+        greet(row, col - 1)
+
+    @pl.when(col < 3)
+    def _():
+        greet(row, col + 1)
+
+    pl.semaphore_wait(barrier, 2 + jnp.minimum(col, 1) + jnp.minimum(3 - col, 1))
+
+    def panel_copy(tile, q, leftward, own=False):
+        part = pl.ds(q * piece, piece)
+        return pltpu.make_async_remote_copy(
+            src_ref=p_ref.at[part] if own else panels.at[tile, part],
+            dst_ref=panels.at[tile, part],
+            send_sem=p_left.at[tile, q] if leftward else p_right.at[tile, q],
+            recv_sem=p_recv.at[tile, q],
+            device_id=(group, row, (col + 3) % 4 if leftward else (col + 1) % 4),
+            device_id_type=MESH,
+        )
+
+    def slab_copy(tile, which, target, own=False):
+        return pltpu.make_async_remote_copy(
+            src_ref=h_ref if own else slabs.at[tile],
+            dst_ref=slabs.at[tile],
+            send_sem=h_send.at[which],
+            recv_sem=h_recv.at[tile],
+            device_id=(group, target, col),
+            device_id_type=MESH,
+        )
+
+    for q in range(CHUNKS):
+        @pl.when(col > 0)
+        def _():
+            panel_copy(col, q, True, True).start()
+
+        @pl.when(col < 3)
+        def _():
+            panel_copy(col, q, False, True).start()
+
+    slab_copy(row, 0, across, True).start()
+    slab_copy(row, 1, sibling, True).start()
+    own_panel = pltpu.make_async_copy(p_ref, panels.at[col], own_sem.at[0])
+    own_slab = pltpu.make_async_copy(h_ref, slabs.at[row], own_sem.at[1])
+    own_panel.start()
+    own_slab.start()
+    clear_corner(right_parts, h_ref.shape[0])
+    own_panel.wait()
+    own_slab.wait()
+
+    def products(index, first):
+        def body(block, acc):
+            start = block * GROUP
+            found = []
+            for k in range(GROUP):
+                found.append(
+                    multiply(
+                        left_parts[slots[index, start + k]],
+                        right_parts[slots[STEPS + index, start + k]],
+                    )
+                )
+            for k in range(GROUP):
+                acc = acc * keep[index, start + k] + found[k]
+                runs[start + k] = acc
+            return acc
+
+        lax.fori_loop(0, width // GROUP, body, jnp.zeros((128, 128), jnp.float32))
+
+        def collect(j, carry):
+            term = runs[last[index, j]] * some[index, j]
+            c_ref[j] = term if first else c_ref[j] + term
+            return carry
+
+        lax.fori_loop(0, c_ref.shape[0], collect, 0)
+
+    def take(distance, q):
+        @pl.when(col + distance <= 3)
+        def _():
+            panel_copy(col + distance, q, True).wait_recv()
+
+            @pl.when(col > 0)
+            def _():
+                panel_copy(col + distance, q, True).start()
+
+        @pl.when(col - distance >= 0)
+        def _():
+            panel_copy(col - distance, q, False).wait_recv()
+
+            @pl.when(col < 3)
+            def _():
+                panel_copy(col - distance, q, False).start()
+
+    split_left(panels.at[col], left_parts, 0, count)
+    split_right(slabs.at[row], right_parts, 0, h_ref.shape[0])
+    products(0, True)
+    for distance in (1, 2):
+        for q in range(CHUNKS):
+            take(distance, q)
+    slab_copy(sibling, 1, sibling).wait_recv()
+    slab_copy(across, 0, across).wait_recv()
+    slab_copy(across, 2, sibling).start()
+    slab_copy(diagonal, 2, sibling).wait_recv()
+    for i in range(1, STEPS):
+        index = jnp.where(col < 2, i, STEPS - i)
+        split_right(slabs.at[(row + index) % 4], right_parts, 0, h_ref.shape[0])
+        for q in range(CHUNKS):
+            if i == 3:
+                take(3, q)
+            split_left(panels.at[(col + index) % 4], left_parts, q * piece, piece)
+        products(index, False)
+
+    for tile in range(4):
+        for q in range(CHUNKS):
+            @pl.when(jnp.logical_and(col > 0, tile >= col))
+            def _():
+                panel_copy(tile, q, True).wait_send()
+
+            @pl.when(jnp.logical_and(col < 3, tile <= col))
+            def _():
+                panel_copy(tile, q, False).wait_send()
+
+    slab_copy(row, 0, across).wait_send()
+    slab_copy(row, 1, sibling).wait_send()
+    slab_copy(across, 2, sibling).wait_send()
+
+
+def ring(p_tiles, h_tiles, pair_lists, pair_counts):
+    slots, last, keep, some = sort_pairs(pair_lists, pair_counts)
+    count, slabs = p_tiles.shape[0], h_tiles.shape[0]
+    dma = pltpu.SemaphoreType.DMA
+    return pl.pallas_call(
+        ring_kernel,
+        out_shape=jax.ShapeDtypeStruct((CAPC, 128, 128), jnp.float32),
+        in_specs=[pl.BlockSpec(memory_space=pltpu.SMEM)] * 4
+        + [pl.BlockSpec(memory_space=pl.ANY)] * 2,
+        out_specs=pl.BlockSpec(memory_space=pltpu.VMEM),
+        scratch_shapes=[
+            pltpu.VMEM((4, count, 128, 128), jnp.float32),
+            pltpu.VMEM((4, slabs, 128, 128), jnp.float32),
+            pltpu.VMEM((count, 128, 256), jnp.bfloat16),
+            pltpu.VMEM((slabs, 256, 256), jnp.bfloat16),
+            pltpu.VMEM((pair_lists.shape[1], 128, 128), jnp.float32),
+            dma((2,)),
+            dma((4, CHUNKS)),
+            dma((4, CHUNKS)),
+            dma((4, CHUNKS)),
+            dma((3,)),
+            dma((4,)),
+        ],
+        compiler_params=pltpu.CompilerParams(
+            collective_id=0, has_side_effects=True, vmem_limit_bytes=48 << 20
+        ),
+        cost_estimate=pl.CostEstimate(
+            flops=STEPS * 96 * 2 * 128 * 256 * 256, bytes_accessed=12 << 20, transcendentals=0
+        ),
+    )(slots, last, keep, some, p_tiles, h_tiles)
+
+
 def shards(p_tiles, h_tiles, pair_lists, pair_counts):
+    if lax.axis_size("row") == 4 and lax.axis_size("col") == 4:
+        return ring(p_tiles, h_tiles, pair_lists, pair_counts)
     accum = jnp.zeros((CAPC, p_tiles.shape[1], p_tiles.shape[2]), jnp.float32)
     panel_tile = p_tiles
     slab_tile = h_tiles

time: 160 us -> 120 us (0.75)
  the two profiles are of different devices: /device:TPU:30 before, /device:TPU:0 now
where the time goes in v2:
time: 120 us
  Pallas kernels  114 us (95%)
  local copies, waits for them, and re-layouts  3.77 us (3%)
  other arithmetic  2.25 us (2%)
    pallas_call x1, Pallas kernels, ring(): pl.pallas_call(ring_kernel, out_shape=jax.ShapeDtypeStruct((CAPC, 128, 12...  114 us
    unnamed x3, local copies, waits for them, and re-layouts  3.07 us

profile of v2, /device:TPU:0, one launch (start us, length us, event | category | flops | bytes accessed | tf_op | source)
XLA Modules:
  0.0 120.2 jit_solution(16008656442552515976)
XLA Ops:
  0.0 0.7 reshape.108
  0.7 0.7 iota_add_fusion
  1.4 0.7 fusion.7
  2.2 0.2 convert_reduce_fusion
  2.4 0.2 select_reduce_fusion
  2.6 0.1 convert_reduce_fusion.1.some
  2.7 0.1 convert_reduce_fusion.2
  2.9 0.1 fusion.5.keep
  3.0 0.0 copy-start
  3.0 1.4 %copy-done = f32[24,128,128]{2,1,0:T(8,128)S(1)} copy-done((f32[24,128,128]{2,1,0:T(8,128)S(1)}, f32[24,128,128]{2,1,0:T(8,128)}, u32[]{:S(2)}) %copy-start) | copy-done | bytes 1572888
  4.4 114.1 %shard_map.49 = f32[48,128,128]{2,1,0:T(8,128)S(1)} custom-call(s32[8,96]{1,0:T(8,128)S(1)} %pad_add_fusion.slots, s32[4,48]{1,0:T(4,128)S(1)} %add_maximum_fusion.last, f32[4,96]{1,0:T(4,128)S(1)} %fusion.5.keep, f32[4,48]{1,0:T(4,128)S(1)} %convert_reduce_fusion.1.some, f32[24,128,128]{2,1,0:T(8,128)S(1)} %copy-done, f32[48,128,128]{2,1,0:T(8,128)} %h_ref.1), custom_call_target="tpu_custom_call" | custom-call | flops 6442450944 | bytes 12582912 | tf_op jit(solution)/shard_map/pallas_call | solution.py:283
  118.5 1.7 %copy.10 = f32[48,128,128]{2,1,0:T(8,128)} copy(f32[48,128,128]{2,1,0:T(8,128)S(1)} %shard_map.49) | data formatting | bytes 6291456
  (4 shorter events, 0.0 us)
Async XLA Ops:
  3.0 1.4 %copy-start = (f32[24,128,128]{2,1,0:T(8,128)S(1)}, f32[24,128,128]{2,1,0:T(8,128)}, u32[]{:S(2)}) copy-start(f32[24,128,128]{2,1,0:T(8,128)} %p_ref.1) | copy-start | bytes 4718596

commit v3 on v2

--- a/solution.py
+++ b/solution.py
@@ -24,14 +24,16 @@
     return high, low
 
 
-def split_left(source, target, first, count):
+def split_left(source, target, first, rows):
+    part = pl.ds(first, rows)
+
     def body(slot, carry):
-        high, low = split(source[slot])
-        target[slot, :, 0:128] = high
-        target[slot, :, 128:256] = low
+        high, low = split(source[slot, part, :])
+        target[slot, part, 0:128] = high
+        target[slot, part, 128:256] = low
         return carry
 
-    lax.fori_loop(first, first + count, body, 0)
+    lax.fori_loop(0, source.shape[0], body, 0)
 
 
 def split_right(source, target, first, count):
@@ -59,7 +61,7 @@
 
 
 def step_kernel(lists, live, left, right, before, after, left_parts, right_parts):
-    split_left(left, left_parts, 0, left.shape[0])
+    split_left(left, left_parts, 0, left.shape[1])
     clear_corner(right_parts, right.shape[0])
     split_right(right, right_parts, 0, right.shape[0])
     after[...] = before[...]
@@ -128,15 +130,14 @@
 
 
 def ring_kernel(
-    slots, last, keep, some, p_ref, h_ref, c_ref,
-    panels, slabs, left_parts, right_parts, runs,
-    own_sem, p_left, p_right, p_recv, h_send, h_recv,
+    slots, last, keep, some, p_ref, h_ref, out_ref,
+    c_ref, panels, slabs, left_parts, right_parts, runs,
+    own_sem, out_sem, p_left, p_right, p_recv, h_send, h_recv,
 ):
     group = lax.axis_index("groups")
     row = lax.axis_index("row")
     col = lax.axis_index("col")
-    count = p_ref.shape[0]
-    piece = count // CHUNKS
+    piece = p_ref.shape[1] // CHUNKS
     width = keep.shape[1]
     sibling = row + 1 - 2 * (row % 2)
     across = (row + 2) % 4
@@ -163,8 +164,8 @@
     def panel_copy(tile, q, leftward, own=False):
         part = pl.ds(q * piece, piece)
         return pltpu.make_async_remote_copy(
-            src_ref=p_ref.at[part] if own else panels.at[tile, part],
-            dst_ref=panels.at[tile, part],
+            src_ref=p_ref.at[:, part] if own else panels.at[tile, :, part],
+            dst_ref=panels.at[tile, :, part],
             send_sem=p_left.at[tile, q] if leftward else p_right.at[tile, q],
             recv_sem=p_recv.at[tile, q],
             device_id=(group, row, (col + 3) % 4 if leftward else (col + 1) % 4),
@@ -200,30 +201,36 @@
     own_panel.wait()
     own_slab.wait()
 
-    def products(index, first):
+    def products(index, first, low, rows):
+        part = pl.ds(low, rows)
+
         def body(block, acc):
             start = block * GROUP
             found = []
             for k in range(GROUP):
                 found.append(
                     multiply(
-                        left_parts[slots[index, start + k]],
+                        left_parts[slots[index, start + k], part, :],
                         right_parts[slots[STEPS + index, start + k]],
                     )
                 )
             for k in range(GROUP):
                 acc = acc * keep[index, start + k] + found[k]
-                runs[start + k] = acc
+                runs[start + k, part, :] = acc
             return acc
 
-        lax.fori_loop(0, width // GROUP, body, jnp.zeros((128, 128), jnp.float32))
+        lax.fori_loop(0, width // GROUP, body, jnp.zeros((rows, 128), jnp.float32))
 
         def collect(j, carry):
-            term = runs[last[index, j]] * some[index, j]
-            c_ref[j] = term if first else c_ref[j] + term
+            term = runs[last[index, j], part, :] * some[index, j]
+            c_ref[j, part, :] = term if first else c_ref[j, part, :] + term
             return carry
 
         lax.fori_loop(0, c_ref.shape[0], collect, 0)
+
+    def out_copy(low, rows, which):
+        part = pl.ds(low, rows)
+        return pltpu.make_async_copy(c_ref.at[:, part], out_ref.at[:, part], out_sem.at[which])
 
     def take(distance, q):
         @pl.when(col + distance <= 3)
@@ -242,9 +249,9 @@
             def _():
                 panel_copy(col - distance, q, False).start()
 
-    split_left(panels.at[col], left_parts, 0, count)
+    split_left(panels.at[col], left_parts, 0, 128)
     split_right(slabs.at[row], right_parts, 0, h_ref.shape[0])
-    products(0, True)
+    products(0, True, 0, 128)
     for distance in (1, 2):
         for q in range(CHUNKS):
             take(distance, q)
@@ -255,11 +262,23 @@
     for i in range(1, STEPS):
         index = jnp.where(col < 2, i, STEPS - i)
         split_right(slabs.at[(row + index) % 4], right_parts, 0, h_ref.shape[0])
-        for q in range(CHUNKS):
-            if i == 3:
-                take(3, q)
-            split_left(panels.at[(col + index) % 4], left_parts, q * piece, piece)
-        products(index, False)
+        left = panels.at[(col + index) % 4]
+        if i < STEPS - 1:
+            split_left(left, left_parts, 0, 128)
+            products(index, False, 0, 128)
+            continue
+        for q in range(CHUNKS - 1):
+            take(3, q)
+        early = 128 - piece
+        split_left(left, left_parts, 0, early)
+        products(index, False, 0, early)
+        out_copy(0, early, 0).start()
+        take(3, CHUNKS - 1)
+        split_left(left, left_parts, early, piece)
+        products(index, False, early, piece)
+        out_copy(early, piece, 1).start()
+        out_copy(0, early, 0).wait()
+        out_copy(early, piece, 1).wait()
 
     for tile in range(4):
         for q in range(CHUNKS):
@@ -285,13 +304,15 @@
         out_shape=jax.ShapeDtypeStruct((CAPC, 128, 128), jnp.float32),
         in_specs=[pl.BlockSpec(memory_space=pltpu.SMEM)] * 4
         + [pl.BlockSpec(memory_space=pl.ANY)] * 2,
-        out_specs=pl.BlockSpec(memory_space=pltpu.VMEM),
+        out_specs=pl.BlockSpec(memory_space=pl.ANY),
         scratch_shapes=[
+            pltpu.VMEM((CAPC, 128, 128), jnp.float32),
             pltpu.VMEM((4, count, 128, 128), jnp.float32),
             pltpu.VMEM((4, slabs, 128, 128), jnp.float32),
             pltpu.VMEM((count, 128, 256), jnp.bfloat16),
             pltpu.VMEM((slabs, 256, 256), jnp.bfloat16),
             pltpu.VMEM((pair_lists.shape[1], 128, 128), jnp.float32),
+            dma((2,)),
             dma((2,)),
             dma((4, CHUNKS)),
             dma((4, CHUNKS)),

time: 120 us -> 119 us (level)
  no operation moved by 1% of the time
where the time goes in v3:
time: 119 us
  Pallas kernels  113 us (95%)
  local copies, waits for them, and re-layouts  3.77 us (3%)
  other arithmetic  2.25 us (2%)
    pallas_call x1, Pallas kernels, ring(): pl.pallas_call(ring_kernel, out_shape=jax.ShapeDtypeStruct((CAPC, 128, 12...  113 us
    unnamed x3, local copies, waits for them, and re-layouts  3.07 us

profile of v3, /device:TPU:0, one launch (start us, length us, event | category | flops | bytes accessed | tf_op | source)
XLA Modules:
  0.0 119.0 jit_solution(9300784191371617504)
XLA Ops:
  0.0 0.7 reshape.108
  0.7 0.7 iota_add_fusion
  1.4 0.7 fusion.7
  2.2 0.2 convert_reduce_fusion
  2.4 0.2 select_reduce_fusion
  2.6 0.1 convert_reduce_fusion.1.some
  2.7 0.1 convert_reduce_fusion.2
  2.9 0.1 fusion.5.keep
  3.0 0.0 copy-start
  3.0 1.4 %copy-done = f32[24,128,128]{2,1,0:T(8,128)S(1)} copy-done((f32[24,128,128]{2,1,0:T(8,128)S(1)}, f32[24,128,128]{2,1,0:T(8,128)}, u32[]{:S(2)}) %copy-start) | copy-done | bytes 1572888
  4.4 113.0 %shard_map.49 = f32[48,128,128]{2,1,0:T(8,128)S(1)} custom-call(s32[8,96]{1,0:T(8,128)S(1)} %pad_add_fusion.slots, s32[4,48]{1,0:T(4,128)S(1)} %add_maximum_fusion.last, f32[4,96]{1,0:T(4,128)S(1)} %fusion.5.keep, f32[4,48]{1,0:T(4,128)S(1)} %convert_reduce_fusion.1.some, f32[24,128,128]{2,1,0:T(8,128)S(1)} %copy-done, f32[48,128,128]{2,1,0:T(8,128)} %h_ref.1), custom_call_target="tpu_custom_call" | custom-call | flops 6442450944 | bytes 12582912 | tf_op jit(solution)/shard_map/pallas_call | solution.py:302
  117.4 1.7 %copy.10 = f32[48,128,128]{2,1,0:T(8,128)} copy(f32[48,128,128]{2,1,0:T(8,128)S(1)} %shard_map.49) | data formatting | bytes 6291456
  (4 shorter events, 0.0 us)
Async XLA Ops:
  3.0 1.4 %copy-start = (f32[24,128,128]{2,1,0:T(8,128)S(1)}, f32[24,128,128]{2,1,0:T(8,128)}, u32[]{:S(2)}) copy-start(f32[24,128,128]{2,1,0:T(8,128)} %p_ref.1) | copy-start | bytes 4718596

commit v4 on v3

--- a/solution.py
+++ b/solution.py
@@ -109,36 +109,47 @@
 MESH = pl.DeviceIdType.MESH
 
 
-def sort_pairs(pair_lists, pair_counts):
-    width = pair_lists.shape[1]
-    triples = pair_lists.reshape(STEPS, 3, width)
-    slot = lax.broadcasted_iota(jnp.int32, (STEPS, width), 1)
-    place = jnp.where(slot < pair_counts, triples[:, 2], CAPC)
+def sort_pairs(lists, count, index, table):
+    width = lists.shape[1]
+    lane = lax.broadcasted_iota(jnp.int32, (width, width), 1)
+    diagonal = lax.broadcasted_iota(jnp.int32, (width, width), 0) == lane
+    slot = lax.broadcasted_iota(jnp.int32, (1, width), 1)
+
+    def column(line):
+        return jnp.sum(jnp.where(diagonal, line, 0), axis=1, keepdims=True)
+
+    def total(mask, values):
+        return jnp.sum(jnp.where(mask, values, 0), axis=0, keepdims=True)
+
+    triple = [lists[3 * index + role : 3 * index + role + 1, :] for role in range(3)]
+    place = jnp.where(slot < count, triple[2], CAPC)
     order = place * width + slot
-    rank = jnp.sum((order[:, None, :] < order[:, :, None]).astype(jnp.int32), axis=2)
-    packed = (triples[:, 0] * 1024 + triples[:, 1]) * 1024 + place
-    hit = rank[:, :, None] == lax.broadcasted_iota(jnp.int32, (STEPS, width, width), 2)
-    ordered = jnp.sum(jnp.where(hit, packed[:, :, None], 0), axis=1)
-    target = ordered % 1024
-    behind = jnp.concatenate([jnp.full((STEPS, 1), -1, jnp.int32), target[:, :-1]], axis=1)
-    keep = (target == behind).astype(jnp.float32)
-    kept = lax.broadcasted_iota(jnp.int32, (STEPS, CAPC, width), 1)
-    last = jnp.sum((place[:, None, :] <= kept).astype(jnp.int32), axis=2) - 1
-    some = jnp.max((place[:, None, :] == kept).astype(jnp.float32), axis=2)
-    slots = jnp.concatenate([ordered // 1048576, ordered // 1024 % 1024], axis=0)
-    return slots, jnp.maximum(last, 0), keep, some
+    rank = jnp.sum((order < column(order)).astype(jnp.int32), axis=1, keepdims=True)
+    place_column = column(place)
+    hit = rank == lane
+    target = total(hit, place_column)
+    behind = jnp.where(slot == 0, -1, total(rank == lane - 1, place_column))
+    lines = (
+        total(hit, column(triple[0])),
+        total(hit, column(triple[1])),
+        (target == behind).astype(jnp.int32),
+        jnp.maximum(total(place_column <= lane, 1) - 1, 0),
+        jnp.minimum(total(place_column == lane, 1), 1),
+    )
+    for role, line in enumerate(lines):
+        table[8 * index + role : 8 * index + role + 1, 0:width] = line
 
 
 def ring_kernel(
-    slots, last, keep, some, p_ref, h_ref, out_ref,
-    c_ref, panels, slabs, left_parts, right_parts, runs,
+    live, lists_ref, p_ref, h_ref, out_ref,
+    lists, table, slots, c_ref, panels, slabs, left_parts, right_parts, runs,
     own_sem, out_sem, p_left, p_right, p_recv, h_send, h_recv,
 ):
     group = lax.axis_index("groups")
     row = lax.axis_index("row")
     col = lax.axis_index("col")
     piece = p_ref.shape[1] // CHUNKS
-    width = keep.shape[1]
+    width = lists_ref.shape[1]
     sibling = row + 1 - 2 * (row % 2)
     across = (row + 2) % 4
     diagonal = (sibling + 2) % 4
@@ -193,11 +204,20 @@
 
     slab_copy(row, 0, across, True).start()
     slab_copy(row, 1, sibling, True).start()
+    own_lists = pltpu.make_async_copy(lists_ref, lists, own_sem.at[2])
+    own_lists.start()
     own_panel = pltpu.make_async_copy(p_ref, panels.at[col], own_sem.at[0])
     own_slab = pltpu.make_async_copy(h_ref, slabs.at[row], own_sem.at[1])
     own_panel.start()
     own_slab.start()
     clear_corner(right_parts, h_ref.shape[0])
+    own_lists.wait()
+    table[...] = jnp.zeros(table.shape, jnp.int32)
+    for index in range(STEPS):
+        sort_pairs(lists, live[index, 0], index, table)
+    moved = pltpu.make_async_copy(table, slots, own_sem.at[3])
+    moved.start()
+    moved.wait()
     own_panel.wait()
     own_slab.wait()
 
@@ -210,19 +230,19 @@
             for k in range(GROUP):
                 found.append(
                     multiply(
-                        left_parts[slots[index, start + k], part, :],
-                        right_parts[slots[STEPS + index, start + k]],
+                        left_parts[slots[8 * index, start + k], part, :],
+                        right_parts[slots[8 * index + 1, start + k]],
                     )
                 )
             for k in range(GROUP):
-                acc = acc * keep[index, start + k] + found[k]
+                acc = acc * slots[8 * index + 2, start + k].astype(jnp.float32) + found[k]
                 runs[start + k, part, :] = acc
             return acc
 
         lax.fori_loop(0, width // GROUP, body, jnp.zeros((rows, 128), jnp.float32))
 
         def collect(j, carry):
-            term = runs[last[index, j], part, :] * some[index, j]
+            term = runs[slots[8 * index + 3, j], part, :] * slots[8 * index + 4, j].astype(jnp.float32)
             c_ref[j, part, :] = term if first else c_ref[j, part, :] + term
             return carry
 
@@ -296,23 +316,25 @@
 
 
 def ring(p_tiles, h_tiles, pair_lists, pair_counts):
-    slots, last, keep, some = sort_pairs(pair_lists, pair_counts)
     count, slabs = p_tiles.shape[0], h_tiles.shape[0]
     dma = pltpu.SemaphoreType.DMA
     return pl.pallas_call(
         ring_kernel,
         out_shape=jax.ShapeDtypeStruct((CAPC, 128, 128), jnp.float32),
-        in_specs=[pl.BlockSpec(memory_space=pltpu.SMEM)] * 4
-        + [pl.BlockSpec(memory_space=pl.ANY)] * 2,
+        in_specs=[pl.BlockSpec(memory_space=pltpu.SMEM)]
+        + [pl.BlockSpec(memory_space=pl.ANY)] * 3,
         out_specs=pl.BlockSpec(memory_space=pl.ANY),
         scratch_shapes=[
+            pltpu.VMEM(pair_lists.shape, jnp.int32),
+            pltpu.VMEM((8 * STEPS, 128), jnp.int32),
+            pltpu.SMEM((8 * STEPS, 128), jnp.int32),
             pltpu.VMEM((CAPC, 128, 128), jnp.float32),
             pltpu.VMEM((4, count, 128, 128), jnp.float32),
             pltpu.VMEM((4, slabs, 128, 128), jnp.float32),
             pltpu.VMEM((count, 128, 256), jnp.bfloat16),
             pltpu.VMEM((slabs, 256, 256), jnp.bfloat16),
             pltpu.VMEM((pair_lists.shape[1], 128, 128), jnp.float32),
-            dma((2,)),
+            dma((4,)),
             dma((2,)),
             dma((4, CHUNKS)),
             dma((4, CHUNKS)),
@@ -326,7 +348,7 @@
         cost_estimate=pl.CostEstimate(
             flops=STEPS * 96 * 2 * 128 * 256 * 256, bytes_accessed=12 << 20, transcendentals=0
         ),
-    )(slots, last, keep, some, p_tiles, h_tiles)
+    )(pair_counts, pair_lists, p_tiles, h_tiles)
 
 
 def shards(p_tiles, h_tiles, pair_lists, pair_counts):

time: 119 us -> 118 us (level)
  other arithmetic: 2.25 us -> 0 us
    unnamed x3 -> x6, local copies, waits for them, and re-layouts: 3.07 us -> 4.51 us
where the time goes in v4:
time: 118 us; the launch traced here: 117 us
  Pallas kernels  113 us (96%)
  local copies, waits for them, and re-layouts  4.51 us (4%)
    pallas_call x1, Pallas kernels, ring(): pl.pallas_call(ring_kernel, out_shape=jax.ShapeDtypeStruct((CAPC, 128, 12...  113 us
    unnamed x6, local copies, waits for them, and re-layouts  4.51 us

profile of v4, /device:TPU:0, one launch (start us, length us, event | category | flops | bytes accessed | tf_op | source)
XLA Modules:
  0.0 117.4 jit_solution(14654439195229226390)
XLA Ops:
  0.0 0.7 copy.5.live
  0.7 0.0 copy-start
  0.7 1.4 %copy-done = f32[24,128,128]{2,1,0:T(8,128)S(1)} copy-done((f32[24,128,128]{2,1,0:T(8,128)S(1)}, f32[24,128,128]{2,1,0:T(8,128)}, u32[]{:S(2)}) %copy-start) | copy-done | bytes 1572888
  2.1 0.0 copy-start.1
  2.2 0.7 copy-done.1
  2.8 112.9 %shard_map.46 = f32[48,128,128]{2,1,0:T(8,128)S(1)} custom-call(s32[4,1]{1,0:T(4,128)S(1)} %copy.5.live, s32[12,96]{1,0:T(8,128)S(1)} %copy-done.1, f32[24,128,128]{2,1,0:T(8,128)S(1)} %copy-done, f32[48,128,128]{2,1,0:T(8,128)} %h_ref.1), custom_call_target="tpu_custom_call" | custom-call | flops 6442450944 | bytes 12582912 | tf_op jit(solution)/shard_map/pallas_call | solution.py:321
  115.8 1.7 %copy.7 = f32[48,128,128]{2,1,0:T(8,128)} copy(f32[48,128,128]{2,1,0:T(8,128)S(1)} %shard_map.46) | data formatting | bytes 6291456
Async XLA Ops:
  0.7 1.4 %copy-start = (f32[24,128,128]{2,1,0:T(8,128)S(1)}, f32[24,128,128]{2,1,0:T(8,128)}, u32[]{:S(2)}) copy-start(f32[24,128,128]{2,1,0:T(8,128)} %p_ref.1) | copy-start | bytes 4718596
  2.1 0.7 copy-start.1

commit v5 on v4

--- a/solution.py
+++ b/solution.py
@@ -141,8 +141,8 @@
 
 
 def ring_kernel(
-    live, lists_ref, p_ref, h_ref, out_ref,
-    lists, table, slots, c_ref, panels, slabs, left_parts, right_parts, runs,
+    live_ref, lists_ref, p_ref, h_ref, out_ref,
+    live, lists, table, slots, c_ref, panels, slabs, left_parts, right_parts, runs,
     own_sem, out_sem, p_left, p_right, p_recv, h_send, h_recv,
 ):
     group = lax.axis_index("groups")
@@ -206,15 +206,18 @@
     slab_copy(row, 1, sibling, True).start()
     own_lists = pltpu.make_async_copy(lists_ref, lists, own_sem.at[2])
     own_lists.start()
+    own_live = pltpu.make_async_copy(live_ref, live, own_sem.at[4])
+    own_live.start()
     own_panel = pltpu.make_async_copy(p_ref, panels.at[col], own_sem.at[0])
     own_slab = pltpu.make_async_copy(h_ref, slabs.at[row], own_sem.at[1])
     own_panel.start()
     own_slab.start()
     clear_corner(right_parts, h_ref.shape[0])
     own_lists.wait()
+    own_live.wait()
     table[...] = jnp.zeros(table.shape, jnp.int32)
     for index in range(STEPS):
-        sort_pairs(lists, live[index, 0], index, table)
+        sort_pairs(lists, live[0, index], index, table)
     moved = pltpu.make_async_copy(table, slots, own_sem.at[3])
     moved.start()
     moved.wait()
@@ -321,10 +324,10 @@
     return pl.pallas_call(
         ring_kernel,
         out_shape=jax.ShapeDtypeStruct((CAPC, 128, 128), jnp.float32),
-        in_specs=[pl.BlockSpec(memory_space=pltpu.SMEM)]
-        + [pl.BlockSpec(memory_space=pl.ANY)] * 3,
+        in_specs=[pl.BlockSpec(memory_space=pltpu.HBM)] * 4,
         out_specs=pl.BlockSpec(memory_space=pl.ANY),
         scratch_shapes=[
+            pltpu.SMEM((1, STEPS), jnp.int32),
             pltpu.VMEM(pair_lists.shape, jnp.int32),
             pltpu.VMEM((8 * STEPS, 128), jnp.int32),
             pltpu.SMEM((8 * STEPS, 128), jnp.int32),
@@ -334,7 +337,7 @@
             pltpu.VMEM((count, 128, 256), jnp.bfloat16),
             pltpu.VMEM((slabs, 256, 256), jnp.bfloat16),
             pltpu.VMEM((pair_lists.shape[1], 128, 128), jnp.float32),
-            dma((4,)),
+            dma((5,)),
             dma((2,)),
             dma((4, CHUNKS)),
             dma((4, CHUNKS)),
@@ -343,12 +346,12 @@
             dma((4,)),
         ],
         compiler_params=pltpu.CompilerParams(
-            collective_id=0, has_side_effects=True, vmem_limit_bytes=48 << 20
+            collective_id=0, has_side_effects=True, vmem_limit_bytes=60 << 20
         ),
         cost_estimate=pl.CostEstimate(
             flops=STEPS * 96 * 2 * 128 * 256 * 256, bytes_accessed=12 << 20, transcendentals=0
         ),
-    )(pair_counts, pair_lists, p_tiles, h_tiles)
+    )(pair_counts.T, pair_lists, p_tiles, h_tiles)
 
 
 def shards(p_tiles, h_tiles, pair_lists, pair_counts):

time: 118 us -> 117 us (level)
    unnamed x6 -> x1, local copies, waits for them, and re-layouts: 4.51 us -> 3.91 us
where the time goes in v5:
time: 117 us
  Pallas kernels  113 us (97%)
  local copies, waits for them, and re-layouts  3.91 us (3%)
    pallas_call x1, Pallas kernels, ring(): pl.pallas_call(ring_kernel, out_shape=jax.ShapeDtypeStruct((CAPC, 128, 12...  113 us
    unnamed x1, local copies, waits for them, and re-layouts  3.91 us

profile of v5, /device:TPU:0, one launch (start us, length us, event | category | flops | bytes accessed | tf_op | source)
XLA Modules:
  0.0 117.3 jit_solution(15366765905549181435)
XLA Ops:
  0.0 113.3 %shard_map.46 = f32[48,128,128]{2,1,0:T(8,128)} custom-call(s32[1,4]{1,0:T(1,128)} %bitcast.1, s32[12,96]{1,0:T(8,128)} %lists_ref.1, f32[24,128,128]{2,1,0:T(8,128)} %p_ref.1, f32[48,128,128]{2,1,0:T(8,128)} %h_ref.1), custom_call_target="tpu_custom_call" | custom-call | flops 6442450944 | bytes 12582912 | tf_op jit(solution)/shard_map/pallas_call | solution.py:324
  113.3 3.9 %copy.6 = f32[48,128,128]{2,1,0:T(8,128)} copy(f32[48,128,128]{2,1,0:T(8,128)} %shard_map.46) | data formatting | bytes 6291456

commit v6 on v5

--- a/solution.py
+++ b/solution.py
@@ -9,7 +9,7 @@
 
 STEPS = 4
 CAPC = 48
-GROUP = 4
+GROUP = 8
 
 
 def from_behind(value, axis, steps):

time: 117 us -> 116 us (level)
    pallas_call x1, Pallas kernels: 113 us -> 112 us  [ring(): pl.pallas_call(ring_kernel, out_shape=jax.ShapeDtypeStruct((CAPC, 128, 12...]
where the time goes in v6:
time: 116 us
  Pallas kernels  112 us (97%)
  local copies, waits for them, and re-layouts  3.91 us (3%)
    pallas_call x1, Pallas kernels, ring(): pl.pallas_call(ring_kernel, out_shape=jax.ShapeDtypeStruct((CAPC, 128, 12...  112 us
    unnamed x1, local copies, waits for them, and re-layouts  3.91 us

profile of v6, /device:TPU:0, one launch (start us, length us, event | category | flops | bytes accessed | tf_op | source)
XLA Modules:
  0.0 116.0 jit_solution(6342756604133957961)
XLA Ops:
  0.0 112.1 %shard_map.46 = f32[48,128,128]{2,1,0:T(8,128)} custom-call(s32[1,4]{1,0:T(1,128)} %bitcast.1, s32[12,96]{1,0:T(8,128)} %lists_ref.1, f32[24,128,128]{2,1,0:T(8,128)} %p_ref.1, f32[48,128,128]{2,1,0:T(8,128)} %h_ref.1), custom_call_target="tpu_custom_call" | custom-call | flops 6442450944 | bytes 12582912 | tf_op jit(solution)/shard_map/pallas_call | solution.py:324
  112.1 3.9 %copy.6 = f32[48,128,128]{2,1,0:T(8,128)} copy(f32[48,128,128]{2,1,0:T(8,128)} %shard_map.46) | data formatting | bytes 6291456
